TPU v7x, 128 devices: a whole 4x4x4 slice. The times are simulated.
128 devices in a mesh: row: 8 (over z, core), col: 16 (over y, x).
Axes of the slice: x: 4, y: 4, z: 4, core: 2. Of those that a mesh axis runs over, the one named last changes fastest.
Arguments:
- tokens: bfloat16 [768, 10240], P('row', 'col'), may hold values from -6 to 6
- weight: bfloat16 [10240, 40960], P('col', 'row'), may hold values from -0.0625 to 0.0625
- upstream: bfloat16 [768, 40960], P('col', 'row'), may hold values from -6 to 6
Outputs:
- grad_input: bfloat16 [768, 10240], P('row', 'col')
- grad_weight: bfloat16 [10240, 40960], P('col', 'row')
All inputs are finite; a program needn't handle non-finite values.
Results may differ from a plain program's by a relative error of at most 0.0049.
Values may be sent and summed in bfloat16 or wider, within the bound.
A program may use at most 128 MiB of HBM per device.

v0:
```python
import jax.numpy as jnp


def gelu_slope(value):
    coeff = 0.7978845608028654
    inner = coeff * (value + 0.044715 * value * value * value)
    tanh_value = jnp.tanh(inner)
    return 0.5 * (1.0 + tanh_value) + 0.5 * value * (1.0 - tanh_value * tanh_value) * coeff * (
        1.0 + 3.0 * 0.044715 * value * value
    )


def reference(tokens, weight, upstream):
    pre = jnp.dot(tokens, weight, preferred_element_type=jnp.float32)
    grad_pre = (upstream.astype(jnp.float32) * gelu_slope(pre)).astype(jnp.bfloat16)
    grad_input = jnp.dot(grad_pre, weight.T, preferred_element_type=jnp.float32).astype(
        jnp.bfloat16
    )
    grad_weight = jnp.dot(tokens.T, grad_pre, preferred_element_type=jnp.float32).astype(
        jnp.bfloat16
    )
    return (grad_input, grad_weight)


def solution(mesh):
    return reference
```

profile of v0, /device:TPU:0, one launch (start us, length us, event | category | flops | bytes accessed | tf_op | source)
XLA Modules:
  0.0 265.1 jit_solution(14169610656954696674)
XLA Ops:
  7.2 0.0 reduce-scatter.7.cloned.1.call-start
  7.2 15.2 %all-gather = bf16[768,640]{1,0:T(8,128)(2,1)S(1)} all-gather(bf16[96,640]{1,0:T(8,128)(2,1)} %param.1), channel_id=1, replica_groups=mesh['axis_0'=8,'axis_1'=16] {'axis_0'}, dimensions={0}, use_global_device_ids=true | all-gather | bytes 1105920 | tf_op args[0]
  22.4 11.9 %fusion.8 = f32[768,5120]{1,0:T(8,128)} fusion(bf16[768,640]{1,0:T(8,128)(2,1)S(1)} %all-gather, bf16[640,5120]{1,0:T(8,128)(2,1)} %param.2), kind=kOutput, calls=%fused_computation.11 | convolution fusion | flops 5033164800 | bytes 23265280 | tf_op jit(solution)/dot_general | solution.py:14
  34.3 0.0 copy-start
  34.3 0.0 reduce-scatter.7.cloned.1.call-update
  34.3 0.0 all-gather.6.cloned.1.call-start
  34.4 106.9 %reduce-scatter.7.cloned.1.call-done = f32[48,5120]{1,0:T(8,128)} async-done(((f32[768,5120]{1,0:T(8,128)}), f32[48,5120]{1,0:T(8,128)}) %reduce-scatter.7.cloned.1.call-update) | async-done | bytes 983056
  141.2 0.0 copy-done
  141.3 2.6 fusion.7
  143.9 0.0 all-gather.6.cloned.1.call-update
  143.9 0.0 reduce-scatter.9.cloned.1.call-start
  144.0 68.0 %all-gather.6.cloned.1.call-done = bf16[768,5120]{1,0:T(8,128)(2,1)} async-done(((bf16[48,5120]{1,0:T(8,128)(2,1)}), bf16[768,5120]{1,0:T(8,128)(2,1)}) %all-gather.6.cloned.1.call-update) | async-done | bytes 7864336 | tf_op jit(solution)/convert_element_type | solution.py:15
  211.9 11.6 %fusion.9 = f32[768,640]{1,0:T(8,128)} fusion(bf16[768,5120]{1,0:T(8,128)(2,1)} %all-gather.6.cloned.1.call-done, bf16[640,5120]{1,0:T(8,128)(2,1)} %param.2), kind=kOutput, calls=%fused_computation.12 | convolution fusion | flops 5033164800 | bytes 16384000 | tf_op jit(solution)/dot_general | solution.py:16
  223.5 0.0 reduce-scatter.9.cloned.1.call-update
  223.5 10.5 %fusion = bf16[640,5120]{0,1:T(8,128)(2,1)} fusion(bf16[768,5120]{1,0:T(8,128)(2,1)} %all-gather.6.cloned.1.call-done, bf16[768,640]{1,0:T(8,128)(2,1)S(1)} %all-gather), kind=kOutput, calls=%fused_computation.1 | convolution fusion | flops 5036441600 | bytes 15400960 | tf_op jit(solution)/dot_general | solution.py:19
  234.0 9.5 %copy = bf16[640,5120]{1,0:T(8,128)(2,1)} copy(bf16[640,5120]{0,1:T(8,128)(2,1)} %fusion) | data formatting | bytes 13107200
  243.5 13.5 %reduce-scatter.9.cloned.1.call-done = f32[96,640]{1,0:T(8,128)} async-done(((f32[768,640]{1,0:T(8,128)}), f32[96,640]{1,0:T(8,128)}) %reduce-scatter.9.cloned.1.call-update) | async-done | bytes 245776
  257.0 1.6 convert_element_type.16
Async XLA Ops:
  7.2 134.1 %reduce-scatter.7.cloned.1.call-start = ((), (), s32[]{:S(2)}) async-start(), calls=%async_computation.3 | async-start | bytes 16711680
  34.3 106.9 %copy-start = (bf16[48,5120]{1,0:T(8,128)(2,1)S(1)}, bf16[48,5120]{1,0:T(8,128)(2,1)}, u32[]{:S(2)}) copy-start(bf16[48,5120]{1,0:T(8,128)(2,1)} %param) | copy-start | bytes 1474564
  34.3 177.6 %all-gather.6.cloned.1.call-start = ((), (), s32[]{:S(2)}) async-start(), calls=%async_computation.2 | async-start | bytes 8355840 | tf_op jit(solution)/convert_element_type | solution.py:15
  143.9 113.1 %reduce-scatter.9.cloned.1.call-start = ((), (), s32[]{:S(2)}) async-start(), calls=%async_computation.4 | async-start | bytes 2211840
Sparse Core Ops, SparseCore 0:
  34.5 106.7 reduce-scatter.6
  144.2 67.6 all-gather.5
  223.6 33.3 reduce-scatter.8
where the time goes:
time: 266 us; the launch traced here: 265 us
  waiting for transfers between devices  188 us (71%)
  matrix products  34 us (13%)
  blocking collectives  15.2 us (6%)
  between operations  13.7 us (5%)
  local copies, waits for them, and re-layouts  9.53 us (4%)
  other arithmetic  4.24 us (2%)
    unnamed x5, waiting for transfers between devices  120 us
    convert_element_type x1, waiting for transfers between devices, reference(): (upstream.astype(jnp.float32) * gelu_slope(pre)).astype(jnp.bfloat16)  68 us
    unnamed x1, blocking collectives  15.2 us
    dot_general x1, matrix products, reference(): pre = jnp.dot(tokens, weight, preferred_element_type=jnp.float32)  11.9 us
    dot_general x1, matrix products, reference(): jnp.dot(grad_pre, weight.T, preferred_element_type=jnp.float32)  11.6 us
    dot_general x1, matrix products, reference(): jnp.dot(tokens.T, grad_pre, preferred_element_type=jnp.float32)  10.5 us
    unnamed x3, local copies, waits for them, and re-layouts  9.53 us
  transfers between devices with their start and end apart: 3, of which 3 were waited for; matrix products, arithmetic and copies ran while one was open for 8% of the time, Pallas kernels for 0%

commit v1 on v0

v1 whole, which is shorter than its diff:
```python
import functools

import jax
import jax.numpy as jnp
from jax import lax
from jax.experimental import pallas as pl
from jax.experimental.pallas import tpu as pltpu
from jax.sharding import PartitionSpec

N_CHUNKS = 10
BF16 = jnp.bfloat16
F32 = jnp.float32
MESH = pl.DeviceIdType.MESH


def gelu_slope(value):
    coeff = 0.7978845608028654
    inner = coeff * (value + 0.044715 * value * value * value)
    tanh_value = jnp.tanh(inner)
    return 0.5 * (1.0 + tanh_value) + 0.5 * value * (1.0 - tanh_value * tanh_value) * coeff * (
        1.0 + 3.0 * 0.044715 * value * value
    )


def mod4(value):
    return lax.rem(value + 4, 4)


def kernel(
    n, part, slab,
    tin, w_hbm, up, gi_out, gw_hbm,
    tok, tok_t, wv, pf, snd1, rcv1, sndc, rcvc, s2, snd2, rcv2, snd2c, rcv2c, g, giacc, gws,
    gx, gt, zs1, zr1, zsc, zrc,
    ssem, rsem, tsem_s, tsem_r, xsem_s, xsem_r, wsem, osem, lsem,
):
    row, col = lax.axis_index("row"), lax.axis_index("col")
    z, core = lax.div(row, 2), lax.rem(row, 2)
    y, x = lax.div(col, 4), lax.rem(col, 4)
    half = part // 2

    def x_dev(d):
        return {"col": y * 4 + mod4(x + d)}

    def y_dev(d):
        return {"col": mod4(y + d) * 4 + x}

    def z_dev(d):
        return {"row": mod4(z + d) * 2 + core}

    sib_dev = {"row": z * 2 + (1 - core)}
    sign = (1, -1)
    major, minor = (x, y), (y, x)
    major_dev, minor_dev = (x_dev, y_dev), (y_dev, x_dev)

    def at(s, m, k):
        return (k, m) if s == 0 else (m, k)

    def w_copy(c):
        return pltpu.make_async_copy(
            w_hbm.at[:, pl.ds(pl.multiple_of(c * 2 * part, 2 * part), 2 * part)], wv.at[c], wsem.at[c]
        )

    for c in range(n):
        w_copy(c).start()
    own_tok = pltpu.make_async_copy(tin, tok.at[z, core], lsem)
    own_tok.start()

    barrier = pltpu.get_barrier_semaphore()
    for dev in (x_dev(1), x_dev(-1), y_dev(1), y_dev(-1), z_dev(1), z_dev(-1), sib_dev):
        pl.semaphore_signal(barrier, inc=1, device_id=dev, device_id_type=MESH)
    pl.semaphore_wait(barrier, 7)

    def t_copy(src, dst, which, dev):
        return pltpu.make_async_remote_copy(
            src_ref=src, dst_ref=dst, send_sem=tsem_s.at[which], recv_sem=tsem_r.at[which],
            device_id=dev, device_id_type=MESH,
        )

    def t_region(which):
        return {
            0: lambda zz, cc: tok.at[zz, cc],
            1: lambda zz, cc: tok.at[zz, cc, 0],
            2: lambda zz, cc: tok.at[zz, cc, 1],
        }[which]

    zm, zp, zo = mod4(z - 1), mod4(z + 1), mod4(z + 2)
    full, lo, hi = t_region(0), t_region(1), t_region(2)
    sends = [
        t_copy(tin, full(z, core), 0, z_dev(1)),
        t_copy(tin, full(z, core), 1, z_dev(-1)),
        t_copy(tin, full(z, core), 2, sib_dev),
    ]
    for cp in sends:
        cp.start()

    def t_wait(region, which):
        t_copy(region, region, which, sib_dev).wait_recv()

    def t_send(region, which, dev):
        cp = t_copy(region, region, which, dev)
        cp.start()
        sends.append(cp)

    t_wait(full(zm, core), 0)
    t_send(lo(zm, core), 3, z_dev(1))
    t_send(full(zm, core), 5, sib_dev)
    t_wait(full(zp, core), 1)
    t_send(hi(zp, core), 4, z_dev(-1))
    t_send(full(zp, core), 6, sib_dev)
    t_wait(lo(zo, core), 3)
    t_send(lo(zo, core), 7, sib_dev)
    t_wait(hi(zo, core), 4)
    t_send(hi(zo, core), 8, sib_dev)
    other = 1 - core
    t_wait(full(z, other), 2)
    t_wait(full(zm, other), 5)
    t_wait(full(zp, other), 6)
    t_wait(lo(zo, other), 7)
    t_wait(hi(zo, other), 8)
    own_tok.wait()

    tokens_all = 16 * slab

    def r_copy(src, dst, kind, c, s, d, dev):
        return pltpu.make_async_remote_copy(
            src_ref=src, dst_ref=dst, send_sem=ssem.at[c, s, kind, d], recv_sem=rsem.at[c, s, kind, d],
            device_id=dev, device_id_type=MESH,
        )

    def r_wait(region, kind, c, s, d):
        r_copy(region, region, kind, c, s, d, sib_dev).wait_recv()

    def s_wait(region, kind, c, s, d):
        r_copy(region, region, kind, c, s, d, sib_dev).wait_send()

    def cols_of(s):
        return slice(s * part, (s + 1) * part)

    def stage0(c):
        slot = lax.rem(c, 3)
        w_copy(c).wait()
        out = jnp.dot(
            tok[...].reshape(tokens_all, tok.shape[-1]), wv[c], preferred_element_type=F32
        )
        pf[slot] = out.reshape(4, 4, slab, 2 * part)
        for s in (0, 1):
            m, cols = major[s], cols_of(s)
            for j in (0, 1):
                def piece(mm, k):
                    a, b = at(s, mm, k)
                    return pf[slot, a, b, :, cols].astype(BF16)

                snd1[c, s, 0, 0, j] = piece(mod4(m + 2), j)
                snd1[c, s, 0, 1, j] = piece(mod4(m + 1), 2 + j)
                snd1[c, s, 1, 0, j] = piece(mod4(m + 2), 2 + j)
                snd1[c, s, 1, 1, j] = piece(mod4(m - 1), j)
            for d in (0, 1):
                r_copy(snd1.at[c, s, d], rcv1.at[c, s, d], 0, c, s, d, major_dev[s](sign[d])).start()

    def stage1(c):
        slot = lax.rem(c, 3)
        for s in (0, 1):
            m, cols = major[s], cols_of(s)
            for d in (0, 1):
                r_wait(rcv1.at[c, s, d], 0, c, s, d)
                for j in (0, 1):
                    a, b = at(s, mod4(m + sign[d]), 2 * d + j)
                    sndc[c, s, d, j] = (
                        pf[slot, a, b, :, cols] + rcv1[c, s, d, 0, j].astype(F32)
                    ).astype(BF16)
                r_copy(sndc.at[c, s, d], rcvc.at[c, s, d], 1, c, s, d, major_dev[s](sign[d])).start()

    def stage2(c):
        slot = lax.rem(c, 3)
        for s in (0, 1):
            m, k, cols = major[s], minor[s], cols_of(s)
            for d in (0, 1):
                r_wait(rcvc.at[c, s, d], 1, c, s, d)
            for kk in range(4):
                a, b = at(s, m, kk)
                h, j = kk // 2, kk % 2
                s2[slot, s, kk] = (
                    pf[slot, a, b, :, cols]
                    + rcvc[c, s, h, j].astype(F32)
                    + rcv1[c, s, 1 - h, 1, j].astype(F32)
                )
            lo_c, hi_c = slice(0, half), slice(half, part)
            snd2[c, s, 0, 0] = s2[slot, s, mod4(k + 2), :, lo_c].astype(BF16)
            snd2[c, s, 0, 1] = s2[slot, s, mod4(k + 1), :, hi_c].astype(BF16)
            snd2[c, s, 1, 0] = s2[slot, s, mod4(k + 2), :, hi_c].astype(BF16)
            snd2[c, s, 1, 1] = s2[slot, s, mod4(k - 1), :, lo_c].astype(BF16)
            for d in (0, 1):
                r_copy(snd2.at[c, s, d], rcv2.at[c, s, d], 2, c, s, d, minor_dev[s](sign[d])).start()

    def stage3(c):
        slot = lax.rem(c, 3)
        for s in (0, 1):
            k = minor[s]
            for d in (0, 1):
                r_wait(rcv2.at[c, s, d], 2, c, s, d)
                cols = slice(d * half, (d + 1) * half)
                snd2c[c, s, d] = (
                    s2[slot, s, mod4(k + sign[d]), :, cols] + rcv2[c, s, d, 0].astype(F32)
                ).astype(BF16)
                r_copy(snd2c.at[c, s, d], rcv2c.at[c, s, d], 3, c, s, d, minor_dev[s](sign[d])).start()

    def stage4(c):
        slot = lax.rem(c, 3)
        for s in (0, 1):
            m, k = major[s], minor[s]
            a, b = at(s, m, k)
            for d in (0, 1):
                r_wait(rcv2c.at[c, s, d], 3, c, s, d)
            for h in (0, 1):
                cols = slice(h * half, (h + 1) * half)
                pre = (
                    s2[slot, s, k, :, cols]
                    + rcv2c[c, s, h].astype(F32)
                    + rcv2[c, s, 1 - h, 1].astype(F32)
                )
                at_col = pl.multiple_of(c * 2 * part + s * part + h * half, half)
                upstream = up[:, pl.ds(at_col, half)].astype(F32)
                g[c, s, a, b, :, cols] = (upstream * gelu_slope(pre)).astype(BF16)
            own = g.at[c, s, a, b]
            for d in (0, 1):
                r_copy(own, own, 4, c, s, d, minor_dev[s](sign[d])).start()

    def near(c, s, d):
        a, b = at(s, major[s], mod4(minor[s] - sign[d]))
        return g.at[c, s, a, b], g.at[c, s, a, b, :, pl.ds(d * half, half)]

    def far(c, s, d):
        a, b = at(s, major[s], mod4(minor[s] + 2))
        return g.at[c, s, a, b, :, pl.ds(d * half, half)]

    def stage5(c):
        for s in (0, 1):
            for d in (0, 1):
                whole, onward = near(c, s, d)
                r_wait(whole, 4, c, s, d)
                r_copy(onward, onward, 5, c, s, d, minor_dev[s](sign[d])).start()

    def line(c, s, m):
        return g.at[c, s, :, m] if s == 0 else g.at[c, s, m]

    def half_line(c, s, m, d):
        return g.at[c, s, pl.ds(2 * d, 2), m] if s == 0 else g.at[c, s, m, pl.ds(2 * d, 2)]

    def stage6(c):
        for s in (0, 1):
            for d in (0, 1):
                r_wait(far(c, s, d), 5, c, s, d)
            own = line(c, s, major[s])
            for d in (0, 1):
                r_copy(own, own, 6, c, s, d, major_dev[s](sign[d])).start()

    def stage7(c):
        for s in (0, 1):
            for d in (0, 1):
                m = mod4(major[s] - sign[d])
                r_wait(line(c, s, m), 6, c, s, d)
                onward = half_line(c, s, m, d)
                r_copy(onward, onward, 7, c, s, d, major_dev[s](sign[d])).start()

    def o_copy(c):
        slot = lax.rem(c, 2)
        return pltpu.make_async_copy(
            gws.at[slot],
            gw_hbm.at[:, pl.ds(pl.multiple_of(c * 2 * part, 2 * part), 2 * part)],
            osem.at[slot],
        )

    def grad_of(c, s):
        return g[c, s].reshape(tokens_all, part)

    def land(c):
        for s in (0, 1):
            for d in (0, 1):
                r_wait(half_line(c, s, mod4(major[s] + 2), d), 7, c, s, d)

    def input_grad(c):
        total = None
        for s in (0, 1):
            term = lax.dot_general(
                grad_of(c, s), wv[c, :, cols_of(s)], (((1,), (1,)), ((), ())), preferred_element_type=F32
            )
            total = term if total is None else total + term
        giacc[...] += total.reshape(giacc.shape)

    def weight_grad(c):
        slot = lax.rem(c, 2)
        for s in (0, 1):
            gws[slot, :, cols_of(s)] = jnp.dot(
                tok_t[...], grad_of(c, s), preferred_element_type=F32
            ).astype(BF16)
        o_copy(c).start()

    def settle(c):
        for s in (0, 1):
            m, k = major[s], minor[s]
            a, b = at(s, m, k)
            for d in (0, 1):
                s_wait(snd1.at[c, s, d], 0, c, s, d)
                s_wait(sndc.at[c, s, d], 1, c, s, d)
                s_wait(snd2.at[c, s, d], 2, c, s, d)
                s_wait(snd2c.at[c, s, d], 3, c, s, d)
                s_wait(g.at[c, s, a, b], 4, c, s, d)
                s_wait(near(c, s, d)[1], 5, c, s, d)
                s_wait(line(c, s, m), 6, c, s, d)
                s_wait(half_line(c, s, mod4(m - sign[d]), d), 7, c, s, d)

    def stage8(c):
        land(c)
        input_grad(c)

        @pl.when(c >= 2)
        def _():
            o_copy(c - 2).wait()

        weight_grad(c)
        settle(c)

    @pl.loop(0, n + 7)
    def _(i):
        for offset, stage in enumerate(
            (stage0, stage1, stage2, stage3, stage4, stage5, stage6, stage7)
        ):
            @pl.when((i >= offset) & (i < n + offset))
            def _(offset=offset, stage=stage):
                stage(i - offset)

            if offset == 0:
                @pl.when(i == 5)
                def _():
                    for cp in sends:
                        cp.wait_send()
                    giacc[...] = jnp.zeros_like(giacc)
                    tok_t[...] = tok[...].reshape(tokens_all, tok.shape[-1]).T

        @pl.when((i >= 8))
        def _():
            stage8(i - 8)

    last = n - 1
    land(last)
    input_grad(last)

    def x_copy(src, dst, which, dev):
        return pltpu.make_async_remote_copy(
            src_ref=src, dst_ref=dst, send_sem=xsem_s.at[which], recv_sem=xsem_r.at[which],
            device_id=dev, device_id_type=MESH,
        )

    cross = x_copy(giacc.at[:, other], gx, 0, sib_dev)
    cross.start()
    o_copy(last - 2).wait()
    weight_grad(last)
    settle(last)
    cross.wait()
    gt[...] = giacc[:, core] + gx[...]
    wire = zs1.dtype
    zs1[0, 0] = gt[zo, 0].astype(wire)
    zs1[0, 1] = gt[zp, 1].astype(wire)
    zs1[1, 0] = gt[zo, 1].astype(wire)
    zs1[1, 1] = gt[zm, 0].astype(wire)
    first = [x_copy(zs1.at[d], zr1.at[d], 1 + d, z_dev(sign[d])) for d in (0, 1)]
    for cp in first:
        cp.start()
    second = []
    for d in (0, 1):
        first[d].wait()
        zsc[d] = (gt[mod4(z + sign[d]), d] + zr1[d, 0].astype(F32)).astype(wire)
        cp = x_copy(zsc.at[d], zrc.at[d], 3 + d, z_dev(sign[d]))
        cp.start()
        second.append(cp)
    for cp in second:
        cp.wait()
    for h in (0, 1):
        gi_out[pl.ds(h * slab, slab), :] = (
            gt[z, h] + zrc[h].astype(F32) + zr1[1 - h, 1].astype(F32)
        ).astype(BF16)
    o_copy(last - 1).wait()
    o_copy(last).wait()


def local(tokens, weight, upstream):
    rows, depth = tokens.shape
    width = weight.shape[1]
    slab = upstream.shape[0]
    n = N_CHUNKS
    part = width // (2 * n)
    half = part // 2
    wire = BF16
    vmem, dma = pltpu.VMEM, pltpu.SemaphoreType.DMA
    scratch = [
        vmem((4, 2, 2, slab, depth), BF16),
        vmem((depth, 16 * slab), BF16),
        vmem((n, depth, 2 * part), BF16),
        vmem((3, 4, 4, slab, 2 * part), F32),
        vmem((n, 2, 2, 2, 2, slab, part), BF16),
        vmem((n, 2, 2, 2, 2, slab, part), BF16),
        vmem((n, 2, 2, 2, slab, part), BF16),
        vmem((n, 2, 2, 2, slab, part), BF16),
        vmem((3, 2, 4, slab, part), F32),
        vmem((n, 2, 2, 2, slab, half), BF16),
        vmem((n, 2, 2, 2, slab, half), BF16),
        vmem((n, 2, 2, slab, half), BF16),
        vmem((n, 2, 2, slab, half), BF16),
        vmem((n, 2, 4, 4, slab, part), BF16),
        vmem((4, 2, 2, slab, depth), F32),
        vmem((2, depth, 2 * part), BF16),
        vmem((4, 2, slab, depth), F32),
        vmem((4, 2, slab, depth), F32),
        vmem((2, 2, slab, depth), wire),
        vmem((2, 2, slab, depth), wire),
        vmem((2, slab, depth), wire),
        vmem((2, slab, depth), wire),
        dma((n, 2, 8, 2)),
        dma((n, 2, 8, 2)),
        dma((9,)),
        dma((9,)),
        dma((5,)),
        dma((5,)),
        dma((n,)),
        dma((2,)),
        dma,
    ]
    return pl.pallas_call(
        functools.partial(kernel, n, part, slab),
        out_shape=(
            jax.ShapeDtypeStruct((rows, depth), BF16),
            jax.ShapeDtypeStruct((depth, width), BF16),
        ),
        in_specs=[
            pl.BlockSpec(memory_space=pltpu.VMEM),
            pl.BlockSpec(memory_space=pl.ANY),
            pl.BlockSpec(memory_space=pltpu.VMEM),
        ],
        out_specs=(
            pl.BlockSpec(memory_space=pltpu.VMEM),
            pl.BlockSpec(memory_space=pl.ANY),
        ),
        scratch_shapes=scratch,
        compiler_params=pltpu.CompilerParams(
            collective_id=0, has_side_effects=True, vmem_limit_bytes=60 * 1024 * 1024
        ),
        cost_estimate=pl.CostEstimate(
            flops=6 * 16 * slab * depth * width, bytes_accessed=4 * depth * width, transcendentals=slab * width
        ),
    )(tokens.reshape(2, rows // 2, depth), weight, upstream)


def solution(mesh):
    spec = PartitionSpec
    return jax.shard_map(
        local,
        mesh=mesh,
        in_specs=(spec("row", "col"), spec("col", "row"), spec("col", "row")),
        out_specs=(spec("row", "col"), spec("col", "row")),
        check_vma=False,
    )
```

time: 266 us -> 129 us (0.48)
  waiting for transfers between devices: 188 us -> 0 us
  Pallas kernels: 0 us -> 120 us
  matrix products: 34 us -> 0 us
  blocking collectives: 15.2 us -> 0 us
  between operations: 13.7 us -> 0.64 us
  other arithmetic: 4.24 us -> 0 us
    unnamed x5 -> x0, waiting for transfers between devices: 120 us -> none
    pallas_call x0 -> x1, Pallas kernels: none -> 120 us  [local(): pl.pallas_call(functools.partial(kernel, n, part, slab), out_shape=(jax.S...]
    convert_element_type x1 -> x0, waiting for transfers between devices: 68 us -> none  [reference(): (upstream.astype(jnp.float32) * gelu_slope(pre)).astype(jnp.bfloat16)]
    dot_general x3 -> x0, matrix products: 34 us -> none  [the longest x1 11.9 us: reference(): pre = jnp.dot(tokens, weight, preferred_element_type=jnp.float32)]
    unnamed x1 -> x0, blocking collectives: 15.2 us -> none
    convert_element_type x2 -> x0, other arithmetic: 4.24 us -> none  [the longest x1 2.63 us: reference(): (upstream.astype(jnp.float32) * gelu_slope(pre)).astype(jnp.bfloat16)]
    unnamed x3 -> x2, local copies, waits for them, and re-layouts: 9.53 us -> 7.64 us
  transfers between devices with their start and end apart: 3 -> 0, of which waited for: 3 -> 0; matrix products, arithmetic and copies ran while one was open for 8% -> 0% of each run, Pallas kernels for 0% -> 0%
where the time goes in v1:
time: 129 us; the launch traced here: 128 us
  Pallas kernels  120 us (93%)
  local copies, waits for them, and re-layouts  7.64 us (6%)
    pallas_call x1, Pallas kernels, local(): pl.pallas_call(functools.partial(kernel, n, part, slab), out_shape=(jax.S...  120 us
    unnamed x2, local copies, waits for them, and re-layouts  7.64 us

profile of v1, /device:TPU:0, one launch (start us, length us, event | category | flops | bytes accessed | tf_op | source)
XLA Modules:
  0.0 128.5 jit_solution(7275642678376017424)
XLA Ops:
  0.6 120.2 %shard_map.50 = (bf16[96,640]{1,0:T(8,128)(2,1)}, bf16[640,5120]{1,0:T(8,128)(2,1)}) custom-call(bf16[2,48,640]{2,1,0:T(8,128)(2,1)} %bitcast.1, bf16[640,5120]{1,0:T(8,128)(2,1)} %w_hbm.1, bf16[48,5120]{1,0:T(8,128)(2,1)} %up.1), custom_call_target="tpu_custom_call" | custom-call | flops 15099494400 | bytes 13107200 | tf_op jit(solution)/shard_map/pallas_call | solution.py:428
  120.8 1.6 %copy.7 = bf16[96,640]{1,0:T(8,128)(2,1)} copy(bf16[96,640]{1,0:T(8,128)(2,1)} %get-tuple-element.4) | data formatting | bytes 245760
  122.4 6.1 %copy.8 = bf16[640,5120]{1,0:T(8,128)(2,1)} copy(bf16[640,5120]{1,0:T(8,128)(2,1)} %get-tuple-element.5) | data formatting | bytes 13107200

commit v2 on v1

--- a/solution.py
+++ b/solution.py
@@ -7,7 +7,7 @@
 from jax.experimental.pallas import tpu as pltpu
 from jax.sharding import PartitionSpec
 
-N_CHUNKS = 10
+N_CHUNKS = 5
 BF16 = jnp.bfloat16
 F32 = jnp.float32
 MESH = pl.DeviceIdType.MESH
@@ -28,10 +28,10 @@
 
 def kernel(
     n, part, slab,
-    tin, w_hbm, up, gi_out, gw_hbm,
-    tok, tok_t, wv, pf, snd1, rcv1, sndc, rcvc, s2, snd2, rcv2, snd2c, rcv2c, g, giacc, gws,
-    gx, gt, zs1, zr1, zsc, zrc,
-    ssem, rsem, tsem_s, tsem_r, xsem_s, xsem_r, wsem, osem, lsem,
+    tin, w_hbm, up_hbm, gi_out, gw_out,
+    up, tok, tok_t, wv, pf, snd1, rcv1, sndc, rcvc, s2, snd2, rcv2, snd2c, rcv2c, g, giacc,
+    gx, zs1, zr1, zsc, zrc,
+    ssem, rsem, tsem_s, tsem_r, xsem_s, xsem_r, wsem, lsem,
 ):
     row, col = lax.axis_index("row"), lax.axis_index("col")
     z, core = lax.div(row, 2), lax.rem(row, 2)
@@ -60,66 +60,79 @@
             w_hbm.at[:, pl.ds(pl.multiple_of(c * 2 * part, 2 * part), 2 * part)], wv.at[c], wsem.at[c]
         )
 
-    for c in range(n):
-        w_copy(c).start()
-    own_tok = pltpu.make_async_copy(tin, tok.at[z, core], lsem)
-    own_tok.start()
-
     barrier = pltpu.get_barrier_semaphore()
     for dev in (x_dev(1), x_dev(-1), y_dev(1), y_dev(-1), z_dev(1), z_dev(-1), sib_dev):
         pl.semaphore_signal(barrier, inc=1, device_id=dev, device_id_type=MESH)
+    own_tok = pltpu.make_async_copy(tin, tok.at[z, core], lsem.at[0])
+    own_tok.start()
+    for c in range(n):
+        w_copy(c).start()
+    own_up = pltpu.make_async_copy(up_hbm, up, lsem.at[1])
+    own_up.start()
+    own_tok.wait()
     pl.semaphore_wait(barrier, 7)
 
-    def t_copy(src, dst, which, dev):
+    def t_copy(region, which, dev):
         return pltpu.make_async_remote_copy(
-            src_ref=src, dst_ref=dst, send_sem=tsem_s.at[which], recv_sem=tsem_r.at[which],
+            src_ref=region, dst_ref=region, send_sem=tsem_s.at[which], recv_sem=tsem_r.at[which],
             device_id=dev, device_id_type=MESH,
         )
 
-    def t_region(which):
-        return {
-            0: lambda zz, cc: tok.at[zz, cc],
-            1: lambda zz, cc: tok.at[zz, cc, 0],
-            2: lambda zz, cc: tok.at[zz, cc, 1],
-        }[which]
+    def full(zz, cc):
+        return tok.at[zz, cc]
+
+    def lo(zz, cc):
+        return tok.at[zz, cc, 0]
+
+    def hi(zz, cc):
+        return tok.at[zz, cc, 1]
 
     zm, zp, zo = mod4(z - 1), mod4(z + 1), mod4(z + 2)
-    full, lo, hi = t_region(0), t_region(1), t_region(2)
-    sends = [
-        t_copy(tin, full(z, core), 0, z_dev(1)),
-        t_copy(tin, full(z, core), 1, z_dev(-1)),
-        t_copy(tin, full(z, core), 2, sib_dev),
-    ]
-    for cp in sends:
-        cp.start()
-
-    def t_wait(region, which):
-        t_copy(region, region, which, sib_dev).wait_recv()
+    other = 1 - core
+    tokens_all = 16 * slab
+    sends = []
 
     def t_send(region, which, dev):
-        cp = t_copy(region, region, which, dev)
+        cp = t_copy(region, which, dev)
         cp.start()
         sends.append(cp)
 
-    t_wait(full(zm, core), 0)
-    t_send(lo(zm, core), 3, z_dev(1))
-    t_send(full(zm, core), 5, sib_dev)
-    t_wait(full(zp, core), 1)
-    t_send(hi(zp, core), 4, z_dev(-1))
-    t_send(full(zp, core), 6, sib_dev)
-    t_wait(lo(zo, core), 3)
-    t_send(lo(zo, core), 7, sib_dev)
-    t_wait(hi(zo, core), 4)
-    t_send(hi(zo, core), 8, sib_dev)
-    other = 1 - core
-    t_wait(full(z, other), 2)
-    t_wait(full(zm, other), 5)
-    t_wait(full(zp, other), 6)
-    t_wait(lo(zo, other), 7)
-    t_wait(hi(zo, other), 8)
-    own_tok.wait()
-
-    tokens_all = 16 * slab
+    def t_wait(region, which):
+        t_copy(region, which, sib_dev).wait_recv()
+
+    def first_pre(zz):
+        rows = tok[zz].reshape(4 * slab, tok.shape[-1])
+        pf[0, zz] = jnp.dot(rows, wv[0], preferred_element_type=F32).reshape(4, slab, 2 * part)
+
+    t_send(lo(z, core), 0, z_dev(1))
+    t_send(hi(z, core), 2, z_dev(-1))
+    t_send(hi(z, core), 1, z_dev(1))
+    t_send(lo(z, core), 3, z_dev(-1))
+    t_send(full(z, core), 4, sib_dev)
+    w_copy(0).wait()
+    t_wait(full(z, other), 4)
+    t_wait(lo(zm, core), 0)
+    t_send(lo(zm, core), 5, z_dev(1))
+    t_wait(hi(zp, core), 2)
+    t_send(hi(zp, core), 6, z_dev(-1))
+    first_pre(z)
+    t_wait(hi(zm, core), 1)
+    t_send(full(zm, core), 7, sib_dev)
+    t_wait(lo(zp, core), 3)
+    t_send(full(zp, core), 8, sib_dev)
+    t_wait(full(zm, other), 7)
+    first_pre(zm)
+    t_wait(lo(zo, core), 5)
+    t_send(lo(zo, core), 9, sib_dev)
+    t_wait(hi(zo, core), 6)
+    t_send(hi(zo, core), 10, sib_dev)
+    t_wait(full(zp, other), 8)
+    first_pre(zp)
+    t_wait(lo(zo, other), 9)
+    t_wait(hi(zo, other), 10)
+    first_pre(zo)
+    own_up.wait()
+
 
     def r_copy(src, dst, kind, c, s, d, dev):
         return pltpu.make_async_remote_copy(
@@ -138,11 +151,15 @@
 
     def stage0(c):
         slot = lax.rem(c, 3)
-        w_copy(c).wait()
-        out = jnp.dot(
-            tok[...].reshape(tokens_all, tok.shape[-1]), wv[c], preferred_element_type=F32
-        )
-        pf[slot] = out.reshape(4, 4, slab, 2 * part)
+
+        @pl.when(c > 0)
+        def _():
+            w_copy(c).wait()
+            out = jnp.dot(
+                tok[...].reshape(tokens_all, tok.shape[-1]), wv[c], preferred_element_type=F32
+            )
+            pf[slot] = out.reshape(4, 4, slab, 2 * part)
+
         for s in (0, 1):
             m, cols = major[s], cols_of(s)
             for j in (0, 1):
@@ -262,14 +279,6 @@
                 onward = half_line(c, s, m, d)
                 r_copy(onward, onward, 7, c, s, d, major_dev[s](sign[d])).start()
 
-    def o_copy(c):
-        slot = lax.rem(c, 2)
-        return pltpu.make_async_copy(
-            gws.at[slot],
-            gw_hbm.at[:, pl.ds(pl.multiple_of(c * 2 * part, 2 * part), 2 * part)],
-            osem.at[slot],
-        )
-
     def grad_of(c, s):
         return g[c, s].reshape(tokens_all, part)
 
@@ -288,12 +297,10 @@
         giacc[...] += total.reshape(giacc.shape)
 
     def weight_grad(c):
-        slot = lax.rem(c, 2)
-        for s in (0, 1):
-            gws[slot, :, cols_of(s)] = jnp.dot(
+        for s in (0, 1):
+            gw_out[:, pl.ds(pl.multiple_of((c * 2 + s) * part, part), part)] = jnp.dot(
                 tok_t[...], grad_of(c, s), preferred_element_type=F32
             ).astype(BF16)
-        o_copy(c).start()
 
     def settle(c):
         for s in (0, 1):
@@ -313,10 +320,6 @@
         land(c)
         input_grad(c)
 
-        @pl.when(c >= 2)
-        def _():
-            o_copy(c - 2).wait()
-
         weight_grad(c)
         settle(c)
 
@@ -343,7 +346,6 @@
 
     last = n - 1
     land(last)
-    input_grad(last)
 
     def x_copy(src, dst, which, dev):
         return pltpu.make_async_remote_copy(
@@ -351,36 +353,57 @@
             device_id=dev, device_id_type=MESH,
         )
 
-    cross = x_copy(giacc.at[:, other], gx, 0, sib_dev)
-    cross.start()
-    o_copy(last - 2).wait()
+    cross = []
+    for which, zz in enumerate((zo, zp, zm, z)):
+        total = None
+        for s in (0, 1):
+            term = lax.dot_general(
+                g[last, s, zz].reshape(4 * slab, part), wv[last, :, cols_of(s)],
+                (((1,), (1,)), ((), ())), preferred_element_type=F32,
+            )
+            total = term if total is None else total + term
+        giacc[zz] += total.reshape(2, 2, slab, total.shape[-1])
+        cp = x_copy(giacc.at[zz, other], gx.at[zz], which, sib_dev)
+        cp.start()
+        cross.append(cp)
+
+    wire = zs1.dtype
+
+    def both_cores(zz, h):
+        return giacc[zz, core, h] + gx[zz, h]
+
+    cross[0].wait()
+    zs1[0, 0] = both_cores(zo, 0).astype(wire)
+    zs1[1, 0] = both_cores(zo, 1).astype(wire)
+    first = [
+        [x_copy(zs1.at[d, ab], zr1.at[d, ab], 4 + 2 * ab + d, z_dev(sign[d])) for d in (0, 1)]
+        for ab in (0, 1)
+    ]
+    first[0][0].start()
+    first[0][1].start()
+    cross[1].wait()
+    zs1[0, 1] = both_cores(zp, 1).astype(wire)
+    first[1][0].start()
+    cross[2].wait()
+    zs1[1, 1] = both_cores(zm, 0).astype(wire)
+    first[1][1].start()
     weight_grad(last)
-    settle(last)
-    cross.wait()
-    gt[...] = giacc[:, core] + gx[...]
-    wire = zs1.dtype
-    zs1[0, 0] = gt[zo, 0].astype(wire)
-    zs1[0, 1] = gt[zp, 1].astype(wire)
-    zs1[1, 0] = gt[zo, 1].astype(wire)
-    zs1[1, 1] = gt[zm, 0].astype(wire)
-    first = [x_copy(zs1.at[d], zr1.at[d], 1 + d, z_dev(sign[d])) for d in (0, 1)]
-    for cp in first:
-        cp.start()
     second = []
     for d in (0, 1):
-        first[d].wait()
-        zsc[d] = (gt[mod4(z + sign[d]), d] + zr1[d, 0].astype(F32)).astype(wire)
-        cp = x_copy(zsc.at[d], zrc.at[d], 3 + d, z_dev(sign[d]))
+        first[0][d].wait()
+        zsc[d] = (both_cores(mod4(z + sign[d]), d) + zr1[d, 0].astype(F32)).astype(wire)
+        cp = x_copy(zsc.at[d], zrc.at[d], 8 + d, z_dev(sign[d]))
         cp.start()
         second.append(cp)
-    for cp in second:
-        cp.wait()
-    for h in (0, 1):
-        gi_out[pl.ds(h * slab, slab), :] = (
-            gt[z, h] + zrc[h].astype(F32) + zr1[1 - h, 1].astype(F32)
+    settle(last)
+    cross[3].wait()
+    for d in (0, 1):
+        first[1][d].wait()
+    for d in (0, 1):
+        second[d].wait()
+        gi_out[pl.ds(d * slab, slab), :] = (
+            both_cores(z, d) + zrc[d].astype(F32) + zr1[1 - d, 1].astype(F32)
         ).astype(BF16)
-    o_copy(last - 1).wait()
-    o_copy(last).wait()
 
 
 def local(tokens, weight, upstream):
@@ -393,6 +416,7 @@
     wire = BF16
     vmem, dma = pltpu.VMEM, pltpu.SemaphoreType.DMA
     scratch = [
+        vmem((slab, width), BF16),
         vmem((4, 2, 2, slab, depth), BF16),
         vmem((depth, 16 * slab), BF16),
         vmem((n, depth, 2 * part), BF16),
@@ -408,8 +432,6 @@
         vmem((n, 2, 2, slab, half), BF16),
         vmem((n, 2, 4, 4, slab, part), BF16),
         vmem((4, 2, 2, slab, depth), F32),
-        vmem((2, depth, 2 * part), BF16),
-        vmem((4, 2, slab, depth), F32),
         vmem((4, 2, slab, depth), F32),
         vmem((2, 2, slab, depth), wire),
         vmem((2, 2, slab, depth), wire),
@@ -417,32 +439,31 @@
         vmem((2, slab, depth), wire),
         dma((n, 2, 8, 2)),
         dma((n, 2, 8, 2)),
-        dma((9,)),
-        dma((9,)),
-        dma((5,)),
-        dma((5,)),
+        dma((11,)),
+        dma((11,)),
+        dma((10,)),
+        dma((10,)),
         dma((n,)),
         dma((2,)),
-        dma,
     ]
     return pl.pallas_call(
         functools.partial(kernel, n, part, slab),
         out_shape=(
-            jax.ShapeDtypeStruct((rows, depth), BF16),
-            jax.ShapeDtypeStruct((depth, width), BF16),
+            pltpu.VMEM((rows, depth), BF16),
+            pltpu.VMEM((depth, width), BF16),
         ),
         in_specs=[
-            pl.BlockSpec(memory_space=pltpu.VMEM),
             pl.BlockSpec(memory_space=pl.ANY),
-            pl.BlockSpec(memory_space=pltpu.VMEM),
+            pl.BlockSpec(memory_space=pl.ANY),
+            pl.BlockSpec(memory_space=pl.ANY),
         ],
         out_specs=(
             pl.BlockSpec(memory_space=pltpu.VMEM),
-            pl.BlockSpec(memory_space=pl.ANY),
+            pl.BlockSpec(memory_space=pltpu.VMEM),
         ),
         scratch_shapes=scratch,
         compiler_params=pltpu.CompilerParams(
-            collective_id=0, has_side_effects=True, vmem_limit_bytes=60 * 1024 * 1024
+            collective_id=0, has_side_effects=True, vmem_limit_bytes=54 * 1024 * 1024
         ),
         cost_estimate=pl.CostEstimate(
             flops=6 * 16 * slab * depth * width, bytes_accessed=4 * depth * width, transcendentals=slab * width

time: 129 us -> 116 us (0.90)
  Pallas kernels: 120 us -> 111 us
  local copies, waits for them, and re-layouts: 7.64 us -> 3.44 us
    pallas_call x1, Pallas kernels: 120 us -> 111 us  [local(): pl.pallas_call(functools.partial(kernel, n, part, slab), out_shape=(pltpu...]
    unnamed x2, local copies, waits for them, and re-layouts: 7.64 us -> 3.44 us
where the time goes in v2:
time: 116 us; the launch traced here: 115 us
  Pallas kernels  111 us (96%)
  local copies, waits for them, and re-layouts  3.44 us (3%)
    pallas_call x1, Pallas kernels, local(): pl.pallas_call(functools.partial(kernel, n, part, slab), out_shape=(pltpu...  111 us
    unnamed x2, local copies, waits for them, and re-layouts  3.44 us

profile of v2, /device:TPU:0, one launch (start us, length us, event | category | flops | bytes accessed | tf_op | source)
XLA Modules:
  0.0 115.5 jit_solution(6095045449402694507)
XLA Ops:
  0.6 111.4 %shard_map.50 = (bf16[96,640]{1,0:T(8,128)(2,1)S(1)}, bf16[640,5120]{1,0:T(8,128)(2,1)S(1)}) custom-call(bf16[2,48,640]{2,1,0:T(8,128)(2,1)} %bitcast.1, bf16[640,5120]{1,0:T(8,128)(2,1)} %w_hbm.1, bf16[48,5120]{1,0:T(8,128)(2,1)} %up_hbm.1), custom_call_target="tpu_custom_call" | custom-call | flops 15099494400 | bytes 13107200 | tf_op jit(solution)/shard_map/pallas_call | solution.py:449
  112.0 0.7 copy.7
  112.7 2.8 %copy.8 = bf16[640,5120]{1,0:T(8,128)(2,1)} copy(bf16[640,5120]{1,0:T(8,128)(2,1)S(1)} %get-tuple-element.3) | data formatting | bytes 13107200

commit v3 on v2

--- a/solution.py
+++ b/solution.py
@@ -8,6 +8,8 @@
 from jax.sharding import PartitionSpec
 
 N_CHUNKS = 5
+EARLY = 2
+FLUSHES = 8
 BF16 = jnp.bfloat16
 F32 = jnp.float32
 MESH = pl.DeviceIdType.MESH
@@ -100,45 +102,72 @@
     def t_wait(region, which):
         t_copy(region, which, sib_dev).wait_recv()
 
-    def first_pre(zz):
+    def r_copy(src, dst, kind, c, s, d, dev):
+        return pltpu.make_async_remote_copy(
+            src_ref=src, dst_ref=dst, send_sem=ssem.at[c, s, kind, d], recv_sem=rsem.at[c, s, kind, d],
+            device_id=dev, device_id_type=MESH,
+        )
+
+    def early(zz):
         rows = tok[zz].reshape(4 * slab, tok.shape[-1])
-        pf[0, zz] = jnp.dot(rows, wv[0], preferred_element_type=F32).reshape(4, slab, 2 * part)
+        h, j = lax.div(zz, 2), lax.rem(zz, 2)
+        q = mod4(zz - y)
+        for c in range(EARLY):
+            pf[c, zz] = jnp.dot(rows, wv[c], preferred_element_type=F32).reshape(4, slab, 2 * part)
+            for d in (0, 1):
+                ab = h if d == 0 else 1 - h
+                owner = mod4(x + 2 - h) if d == 0 else mod4(x + 3 - h)
+                piece = snd1.at[c, 0, d, ab, j]
+                piece[...] = pf[c, zz, owner, :, :part].astype(BF16)
+                r_copy(piece, rcv1.at[c, 0, d, ab, j], 0, c, 0, d, x_dev(sign[d])).start()
+
+            def unit(d, ab, k0, c=c):
+                snd1[c, 1, d, ab] = pf[c, zz, k0:k0 + 2, :, part:].astype(BF16)
+                r_copy(snd1.at[c, 1, d, ab], rcv1.at[c, 1, d, ab], 0, c, 1, d, y_dev(sign[d])).start()
+
+            @pl.when(q == 1)
+            def _():
+                unit(0, 1, 2)
+
+            @pl.when(q == 2)
+            def _():
+                unit(0, 0, 0)
+                unit(1, 0, 2)
+
+            @pl.when(q == 3)
+            def _():
+                unit(1, 1, 0)
 
     t_send(lo(z, core), 0, z_dev(1))
     t_send(hi(z, core), 2, z_dev(-1))
     t_send(hi(z, core), 1, z_dev(1))
     t_send(lo(z, core), 3, z_dev(-1))
     t_send(full(z, core), 4, sib_dev)
-    w_copy(0).wait()
+    for c in range(EARLY):
+        w_copy(c).wait()
     t_wait(full(z, other), 4)
     t_wait(lo(zm, core), 0)
     t_send(lo(zm, core), 5, z_dev(1))
     t_wait(hi(zp, core), 2)
     t_send(hi(zp, core), 6, z_dev(-1))
-    first_pre(z)
+    early(z)
     t_wait(hi(zm, core), 1)
     t_send(full(zm, core), 7, sib_dev)
     t_wait(lo(zp, core), 3)
     t_send(full(zp, core), 8, sib_dev)
     t_wait(full(zm, other), 7)
-    first_pre(zm)
+    early(zm)
     t_wait(lo(zo, core), 5)
     t_send(lo(zo, core), 9, sib_dev)
     t_wait(hi(zo, core), 6)
     t_send(hi(zo, core), 10, sib_dev)
     t_wait(full(zp, other), 8)
-    first_pre(zp)
+    early(zp)
     t_wait(lo(zo, other), 9)
     t_wait(hi(zo, other), 10)
-    first_pre(zo)
+    early(zo)
     own_up.wait()
 
-
-    def r_copy(src, dst, kind, c, s, d, dev):
-        return pltpu.make_async_remote_copy(
-            src_ref=src, dst_ref=dst, send_sem=ssem.at[c, s, kind, d], recv_sem=rsem.at[c, s, kind, d],
-            device_id=dev, device_id_type=MESH,
-        )
 
     def r_wait(region, kind, c, s, d):
         r_copy(region, region, kind, c, s, d, sib_dev).wait_recv()
@@ -152,14 +181,11 @@
     def stage0(c):
         slot = lax.rem(c, 3)
 
-        @pl.when(c > 0)
-        def _():
-            w_copy(c).wait()
-            out = jnp.dot(
-                tok[...].reshape(tokens_all, tok.shape[-1]), wv[c], preferred_element_type=F32
-            )
-            pf[slot] = out.reshape(4, 4, slab, 2 * part)
-
+        w_copy(c).wait()
+        out = jnp.dot(
+            tok[...].reshape(tokens_all, tok.shape[-1]), wv[c], preferred_element_type=F32
+        )
+        pf[slot] = out.reshape(4, 4, slab, 2 * part)
         for s in (0, 1):
             m, cols = major[s], cols_of(s)
             for j in (0, 1):
@@ -323,12 +349,14 @@
         weight_grad(c)
         settle(c)
 
-    @pl.loop(0, n + 7)
+    @pl.loop(1, n + 7)
     def _(i):
         for offset, stage in enumerate(
             (stage0, stage1, stage2, stage3, stage4, stage5, stage6, stage7)
         ):
-            @pl.when((i >= offset) & (i < n + offset))
+            start = EARLY if offset == 0 else 0
+
+            @pl.when((i >= offset + start) & (i < n + offset))
             def _(offset=offset, stage=stage):
                 stage(i - offset)
 
@@ -404,6 +432,18 @@
         gi_out[pl.ds(d * slab, slab), :] = (
             both_cores(z, d) + zrc[d].astype(F32) + zr1[1 - d, 1].astype(F32)
         ).astype(BF16)
+
+
+def flush(gi, gw, gi_out, gw_out, sem):
+    step = gw.shape[0] // FLUSHES
+    copies = [pltpu.make_async_copy(gi, gi_out, sem.at[FLUSHES])]
+    for j in range(FLUSHES):
+        rows = pl.ds(j * step, step)
+        copies.append(pltpu.make_async_copy(gw.at[rows], gw_out.at[rows], sem.at[j]))
+    for cp in copies:
+        cp.start()
+    for cp in copies:
+        cp.wait()
 
 
 def local(tokens, weight, upstream):
@@ -446,7 +486,7 @@
         dma((n,)),
         dma((2,)),
     ]
-    return pl.pallas_call(
+    gi, gw = pl.pallas_call(
         functools.partial(kernel, n, part, slab),
         out_shape=(
             pltpu.VMEM((rows, depth), BF16),
@@ -470,6 +510,18 @@
         ),
     )(tokens.reshape(2, rows // 2, depth), weight, upstream)
 
+    return pl.pallas_call(
+        flush,
+        out_shape=(
+            jax.ShapeDtypeStruct((rows, depth), BF16),
+            jax.ShapeDtypeStruct((depth, width), BF16),
+        ),
+        in_specs=[pl.BlockSpec(memory_space=pltpu.VMEM)] * 2,
+        out_specs=(pl.BlockSpec(memory_space=pl.ANY),) * 2,
+        scratch_shapes=[dma((FLUSHES + 1,))],
+        compiler_params=pltpu.CompilerParams(vmem_limit_bytes=1024 * 1024),
+    )(pltpu.with_memory_space_constraint(gi, pltpu.VMEM), pltpu.with_memory_space_constraint(gw, pltpu.VMEM))
+
 
 def solution(mesh):
     spec = PartitionSpec

time: 116 us -> 114 us (0.983)
  local copies, waits for them, and re-layouts: 3.44 us -> 0 us
  Pallas kernels: 111 us -> 113 us
    unnamed x2 -> x0, local copies, waits for them, and re-layouts: 3.44 us -> none
    pallas_call x0 -> x1, Pallas kernels: none -> 2.85 us  [local(): pl.pallas_call(flush, out_shape=(jax.ShapeDtypeStruct((rows, depth), BF16...]
    pallas_call x1, Pallas kernels: 111 us -> 110 us  [local(): pl.pallas_call(functools.partial(kernel, n, part, slab), out_shape=(pltpu...]
where the time goes in v3:
time: 114 us
  Pallas kernels  113 us (99%)
    pallas_call x1, Pallas kernels, local(): pl.pallas_call(functools.partial(kernel, n, part, slab), out_shape=(pltpu...  110 us
    pallas_call x1, Pallas kernels, local(): pl.pallas_call(flush, out_shape=(jax.ShapeDtypeStruct((rows, depth), BF16...  2.85 us

profile of v3, /device:TPU:0, one launch (start us, length us, event | category | flops | bytes accessed | tf_op | source)
XLA Modules:
  0.0 113.6 jit_solution(182848843197416733)
XLA Ops:
  0.6 110.1 %shard_map.50 = (bf16[96,640]{1,0:T(8,128)(2,1)S(1)}, bf16[640,5120]{1,0:T(8,128)(2,1)S(1)}) custom-call(bf16[2,48,640]{2,1,0:T(8,128)(2,1)} %bitcast.1, bf16[640,5120]{1,0:T(8,128)(2,1)} %w_hbm.1, bf16[48,5120]{1,0:T(8,128)(2,1)} %up_hbm.1), custom_call_target="tpu_custom_call" | custom-call | flops 15099494400 | bytes 13107200 | tf_op jit(solution)/shard_map/pallas_call | solution.py:489
  110.7 2.9 %shard_map.51 = (bf16[96,640]{1,0:T(8,128)(2,1)}, bf16[640,5120]{1,0:T(8,128)(2,1)}) custom-call(bf16[96,640]{1,0:T(8,128)(2,1)S(1)} %get-tuple-element.4.gi, bf16[640,5120]{1,0:T(8,128)(2,1)S(1)} %get-tuple-element.5.gw), custom_call_target="tpu_custom_call" | custom-call | tf_op jit(solution)/shard_map/pallas_call | solution.py:513

commit v4 on v3

--- a/solution.py
+++ b/solution.py
@@ -185,13 +185,13 @@
         out = jnp.dot(
             tok[...].reshape(tokens_all, tok.shape[-1]), wv[c], preferred_element_type=F32
         )
-        pf[slot] = out.reshape(4, 4, slab, 2 * part)
+        pf[lax.rem(c, 4)] = out.reshape(4, 4, slab, 2 * part)
         for s in (0, 1):
             m, cols = major[s], cols_of(s)
             for j in (0, 1):
                 def piece(mm, k):
                     a, b = at(s, mm, k)
-                    return pf[slot, a, b, :, cols].astype(BF16)
+                    return pf[lax.rem(c, 4), a, b, :, cols].astype(BF16)
 
                 snd1[c, s, 0, 0, j] = piece(mod4(m + 2), j)
                 snd1[c, s, 0, 1, j] = piece(mod4(m + 1), 2 + j)
@@ -209,7 +209,7 @@
                 for j in (0, 1):
                     a, b = at(s, mod4(m + sign[d]), 2 * d + j)
                     sndc[c, s, d, j] = (
-                        pf[slot, a, b, :, cols] + rcv1[c, s, d, 0, j].astype(F32)
+                        pf[lax.rem(c, 4), a, b, :, cols] + rcv1[c, s, d, 0, j].astype(F32)
                     ).astype(BF16)
                 r_copy(sndc.at[c, s, d], rcvc.at[c, s, d], 1, c, s, d, major_dev[s](sign[d])).start()
 
@@ -223,7 +223,7 @@
                 a, b = at(s, m, kk)
                 h, j = kk // 2, kk % 2
                 s2[slot, s, kk] = (
-                    pf[slot, a, b, :, cols]
+                    pf[lax.rem(c, 4), a, b, :, cols]
                     + rcvc[c, s, h, j].astype(F32)
                     + rcv1[c, s, 1 - h, 1, j].astype(F32)
                 )
@@ -349,16 +349,17 @@
         weight_grad(c)
         settle(c)
 
-    @pl.loop(1, n + 7)
+    @pl.loop(1, n + 6)
     def _(i):
         for offset, stage in enumerate(
             (stage0, stage1, stage2, stage3, stage4, stage5, stage6, stage7)
         ):
+            shift = offset if offset else -1
             start = EARLY if offset == 0 else 0
 
-            @pl.when((i >= offset + start) & (i < n + offset))
-            def _(offset=offset, stage=stage):
-                stage(i - offset)
+            @pl.when((i >= shift + start) & (i < n + shift))
+            def _(shift=shift, stage=stage):
+                stage(i - shift)
 
             if offset == 0:
                 @pl.when(i == 5)
@@ -373,6 +374,9 @@
             stage8(i - 8)
 
     last = n - 1
+    stage7(last)
+    land(last - 1)
+    input_grad(last - 1)
     land(last)
 
     def x_copy(src, dst, which, dev):
@@ -415,7 +419,7 @@
     cross[2].wait()
     zs1[1, 1] = both_cores(zm, 0).astype(wire)
     first[1][1].start()
-    weight_grad(last)
+    weight_grad(last - 1)
     second = []
     for d in (0, 1):
         first[0][d].wait()
@@ -423,6 +427,8 @@
         cp = x_copy(zsc.at[d], zrc.at[d], 8 + d, z_dev(sign[d]))
         cp.start()
         second.append(cp)
+    weight_grad(last)
+    settle(last - 1)
     settle(last)
     cross[3].wait()
     for d in (0, 1):
@@ -460,7 +466,7 @@
         vmem((4, 2, 2, slab, depth), BF16),
         vmem((depth, 16 * slab), BF16),
         vmem((n, depth, 2 * part), BF16),
-        vmem((3, 4, 4, slab, 2 * part), F32),
+        vmem((4, 4, 4, slab, 2 * part), F32),
         vmem((n, 2, 2, 2, 2, slab, part), BF16),
         vmem((n, 2, 2, 2, 2, slab, part), BF16),
         vmem((n, 2, 2, 2, slab, part), BF16),
@@ -503,7 +509,7 @@
         ),
         scratch_shapes=scratch,
         compiler_params=pltpu.CompilerParams(
-            collective_id=0, has_side_effects=True, vmem_limit_bytes=54 * 1024 * 1024
+            collective_id=0, has_side_effects=True, vmem_limit_bytes=56 * 1024 * 1024 + 512 * 1024
         ),
         cost_estimate=pl.CostEstimate(
             flops=6 * 16 * slab * depth * width, bytes_accessed=4 * depth * width, transcendentals=slab * width

time: 114 us -> 113 us (level)
    pallas_call x1, Pallas kernels: 110 us -> 109 us  [local(): pl.pallas_call(functools.partial(kernel, n, part, slab), out_shape=(pltpu...]
where the time goes in v4:
time: 113 us; the launch traced here: 112 us
  Pallas kernels  112 us (99%)
    pallas_call x1, Pallas kernels, local(): pl.pallas_call(functools.partial(kernel, n, part, slab), out_shape=(pltpu...  109 us
    pallas_call x1, Pallas kernels, local(): pl.pallas_call(flush, out_shape=(jax.ShapeDtypeStruct((rows, depth), BF16...  2.85 us

profile of v4, /device:TPU:0, one launch (start us, length us, event | category | flops | bytes accessed | tf_op | source)
XLA Modules:
  0.0 112.4 jit_solution(3490253149673075645)
XLA Ops:
  0.6 108.9 %shard_map.50 = (bf16[96,640]{1,0:T(8,128)(2,1)S(1)}, bf16[640,5120]{1,0:T(8,128)(2,1)S(1)}) custom-call(bf16[2,48,640]{2,1,0:T(8,128)(2,1)} %bitcast.1, bf16[640,5120]{1,0:T(8,128)(2,1)} %w_hbm.1, bf16[48,5120]{1,0:T(8,128)(2,1)} %up_hbm.1), custom_call_target="tpu_custom_call" | custom-call | flops 15099494400 | bytes 13107200 | tf_op jit(solution)/shard_map/pallas_call | solution.py:495
  109.5 2.9 %shard_map.51 = (bf16[96,640]{1,0:T(8,128)(2,1)}, bf16[640,5120]{1,0:T(8,128)(2,1)}) custom-call(bf16[96,640]{1,0:T(8,128)(2,1)S(1)} %get-tuple-element.4.gi, bf16[640,5120]{1,0:T(8,128)(2,1)S(1)} %get-tuple-element.5.gw), custom_call_target="tpu_custom_call" | custom-call | tf_op jit(solution)/shard_map/pallas_call | solution.py:519

commit v5 on v4

--- a/solution.py
+++ b/solution.py
@@ -71,12 +71,11 @@
         w_copy(c).start()
     own_up = pltpu.make_async_copy(up_hbm, up, lsem.at[1])
     own_up.start()
-    own_tok.wait()
     pl.semaphore_wait(barrier, 7)
 
-    def t_copy(region, which, dev):
+    def t_copy(region, which, dev, src=None):
         return pltpu.make_async_remote_copy(
-            src_ref=region, dst_ref=region, send_sem=tsem_s.at[which], recv_sem=tsem_r.at[which],
+            src_ref=region if src is None else src, dst_ref=region, send_sem=tsem_s.at[which], recv_sem=tsem_r.at[which],
             device_id=dev, device_id_type=MESH,
         )
 
@@ -94,8 +93,8 @@
     tokens_all = 16 * slab
     sends = []
 
-    def t_send(region, which, dev):
-        cp = t_copy(region, which, dev)
+    def t_send(region, which, dev, src=None):
+        cp = t_copy(region, which, dev, src)
         cp.start()
         sends.append(cp)
 
@@ -138,11 +137,15 @@
             def _():
                 unit(1, 1, 0)
 
-    t_send(lo(z, core), 0, z_dev(1))
-    t_send(hi(z, core), 2, z_dev(-1))
-    t_send(hi(z, core), 1, z_dev(1))
-    t_send(lo(z, core), 3, z_dev(-1))
-    t_send(full(z, core), 4, sib_dev)
+    for src, dst, which, dev in (
+        (tin.at[0], lo(z, core), 0, z_dev(1)),
+        (tin.at[1], hi(z, core), 2, z_dev(-1)),
+        (tin.at[1], hi(z, core), 1, z_dev(1)),
+        (tin.at[0], lo(z, core), 3, z_dev(-1)),
+        (tin, full(z, core), 4, sib_dev),
+    ):
+        t_send(dst, which, dev, src)
+    own_tok.wait()
     for c in range(EARLY):
         w_copy(c).wait()
     t_wait(full(z, other), 4)
@@ -362,7 +365,7 @@
                 stage(i - shift)
 
             if offset == 0:
-                @pl.when(i == 5)
+                @pl.when(i == 3)
                 def _():
                     for cp in sends:
                         cp.wait_send()

time: 113 us -> 112 us (level)
  no operation moved by 1% of the time
where the time goes in v5:
time: 112 us
  Pallas kernels  112 us (100%)
    pallas_call x1, Pallas kernels, local(): pl.pallas_call(functools.partial(kernel, n, part, slab), out_shape=(pltpu...  109 us
    pallas_call x1, Pallas kernels, local(): pl.pallas_call(flush, out_shape=(jax.ShapeDtypeStruct((rows, depth), BF16...  2.85 us

profile of v5, /device:TPU:0, one launch (start us, length us, event | category | flops | bytes accessed | tf_op | source)
XLA Modules:
  0.0 112.1 jit_solution(6757528528853587607)
XLA Ops:
  0.6 108.7 %shard_map.50 = (bf16[96,640]{1,0:T(8,128)(2,1)S(1)}, bf16[640,5120]{1,0:T(8,128)(2,1)S(1)}) custom-call(bf16[2,48,640]{2,1,0:T(8,128)(2,1)} %bitcast.1, bf16[640,5120]{1,0:T(8,128)(2,1)} %w_hbm.1, bf16[48,5120]{1,0:T(8,128)(2,1)} %up_hbm.1), custom_call_target="tpu_custom_call" | custom-call | flops 15099494400 | bytes 13107200 | tf_op jit(solution)/shard_map/pallas_call | solution.py:498
  109.3 2.9 %shard_map.51 = (bf16[96,640]{1,0:T(8,128)(2,1)}, bf16[640,5120]{1,0:T(8,128)(2,1)}) custom-call(bf16[96,640]{1,0:T(8,128)(2,1)S(1)} %get-tuple-element.4.gi, bf16[640,5120]{1,0:T(8,128)(2,1)S(1)} %get-tuple-element.5.gw), custom_call_target="tpu_custom_call" | custom-call | tf_op jit(solution)/shard_map/pallas_call | solution.py:522

commit v6 on v5

--- a/solution.py
+++ b/solution.py
@@ -149,11 +149,11 @@
     for c in range(EARLY):
         w_copy(c).wait()
     t_wait(full(z, other), 4)
+    early(z)
     t_wait(lo(zm, core), 0)
     t_send(lo(zm, core), 5, z_dev(1))
     t_wait(hi(zp, core), 2)
     t_send(hi(zp, core), 6, z_dev(-1))
-    early(z)
     t_wait(hi(zm, core), 1)
     t_send(full(zm, core), 7, sib_dev)
     t_wait(lo(zp, core), 3)
@@ -296,16 +296,17 @@
         for s in (0, 1):
             for d in (0, 1):
                 r_wait(far(c, s, d), 5, c, s, d)
-            own = line(c, s, major[s])
-            for d in (0, 1):
-                r_copy(own, own, 6, c, s, d, major_dev[s](sign[d])).start()
+            for turn, kind in ((0, 6), (1, 8)):
+                for d in (0, 1):
+                    own = half_line(c, s, major[s], d if turn == 0 else 1 - d)
+                    r_copy(own, own, kind, c, s, d, major_dev[s](sign[d])).start()
 
     def stage7(c):
         for s in (0, 1):
             for d in (0, 1):
                 m = mod4(major[s] - sign[d])
-                r_wait(line(c, s, m), 6, c, s, d)
                 onward = half_line(c, s, m, d)
+                r_wait(onward, 6, c, s, d)
                 r_copy(onward, onward, 7, c, s, d, major_dev[s](sign[d])).start()
 
     def grad_of(c, s):
@@ -314,6 +315,7 @@
     def land(c):
         for s in (0, 1):
             for d in (0, 1):
+                r_wait(half_line(c, s, mod4(major[s] - sign[d]), 1 - d), 8, c, s, d)
                 r_wait(half_line(c, s, mod4(major[s] + 2), d), 7, c, s, d)
 
     def input_grad(c):
@@ -342,7 +344,8 @@
                 s_wait(snd2c.at[c, s, d], 3, c, s, d)
                 s_wait(g.at[c, s, a, b], 4, c, s, d)
                 s_wait(near(c, s, d)[1], 5, c, s, d)
-                s_wait(line(c, s, m), 6, c, s, d)
+                s_wait(half_line(c, s, m, d), 6, c, s, d)
+                s_wait(half_line(c, s, m, 1 - d), 8, c, s, d)
                 s_wait(half_line(c, s, mod4(m - sign[d]), d), 7, c, s, d)
 
     def stage8(c):
@@ -486,8 +489,8 @@
         vmem((2, 2, slab, depth), wire),
         vmem((2, slab, depth), wire),
         vmem((2, slab, depth), wire),
-        dma((n, 2, 8, 2)),
-        dma((n, 2, 8, 2)),
+        dma((n, 2, 9, 2)),
+        dma((n, 2, 9, 2)),
         dma((11,)),
         dma((11,)),
         dma((10,)),

time: 112 us -> 112 us (level)
  no operation moved by 1% of the time
where the time goes in v6:
time: 112 us
  Pallas kernels  111 us (99%)
    pallas_call x1, Pallas kernels, local(): pl.pallas_call(functools.partial(kernel, n, part, slab), out_shape=(pltpu...  108 us
    pallas_call x1, Pallas kernels, local(): pl.pallas_call(flush, out_shape=(jax.ShapeDtypeStruct((rows, depth), BF16...  2.85 us

profile of v6, /device:TPU:0, one launch (start us, length us, event | category | flops | bytes accessed | tf_op | source)
XLA Modules:
  0.0 111.6 jit_solution(3128585417230728281)
XLA Ops:
  0.6 108.0 %shard_map.50 = (bf16[96,640]{1,0:T(8,128)(2,1)S(1)}, bf16[640,5120]{1,0:T(8,128)(2,1)S(1)}) custom-call(bf16[2,48,640]{2,1,0:T(8,128)(2,1)} %bitcast.1, bf16[640,5120]{1,0:T(8,128)(2,1)} %w_hbm.1, bf16[48,5120]{1,0:T(8,128)(2,1)} %up_hbm.1), custom_call_target="tpu_custom_call" | custom-call | flops 15099494400 | bytes 13107200 | tf_op jit(solution)/shard_map/pallas_call | solution.py:501
  108.6 2.9 %shard_map.51 = (bf16[96,640]{1,0:T(8,128)(2,1)}, bf16[640,5120]{1,0:T(8,128)(2,1)}) custom-call(bf16[96,640]{1,0:T(8,128)(2,1)S(1)} %get-tuple-element.4.gi, bf16[640,5120]{1,0:T(8,128)(2,1)S(1)} %get-tuple-element.5.gw), custom_call_target="tpu_custom_call" | custom-call | tf_op jit(solution)/shard_map/pallas_call | solution.py:525
